TPU v7x, 32 devices: a whole 2x2x4 slice. The times are simulated.
32 devices in a mesh: groups: 2 (over y), rows: 4 (over x, core), mods: 4 (over z).
Axes of the slice: x: 2, y: 2, z: 4, core: 2. Of those that a mesh axis runs over, the one named last changes fastest.
Arguments:
- query_grads: float32 [512, 16, 1024], P(('groups', 'rows'), 'mods'), parts along dimension 0, may hold values from -6 to 6
- train_grads: bfloat16 [8192, 16, 1024], P(('groups', 'rows'), 'mods'), parts along dimension 0, may hold values from -48 to 48
- token_counts: int32 [8192], P(('groups', 'rows')), parts along dimension 0, may hold values from 256 to 2048
- query_owner: int32 [512], P('groups'), parts along dimension 0, may hold values from 0 to 255, each once
- module_map: int32 [16], replicated, may hold values from 0 to 15, each once
- out_basis: float32 [16, 32, 32], replicated, may hold values from -1 to 1
- in_basis: float32 [16, 32, 32], replicated, may hold values from -1 to 1
- eigen_values: float32 [16, 1024], replicated, may hold values from 0.05 to 5
Outputs:
- scores: float32 [512, 4096], P(('groups', 'mods'), 'rows'), parts along dimension 0
There are 2 independent parts, one for each index of `groups`. A program takes and returns all parts, laid end to end along the dimension named above; an argument that names none is the same for every part. Nothing has to cross between parts.
Inputs may be any that keep to these rules, and one draw needn't show every extreme that they name: `query_owner`: each query id stands in exactly one slot. `module_map`: each module stands in exactly one slot.
All inputs are finite; a program needn't handle non-finite values.
Results may differ from a plain program's by a relative error of at most 0.0038.
Values may be sent and summed in bfloat16 or wider, within the bound.
A program may use at most 192 MiB of HBM per device.

v0:
```python
import jax
import jax.numpy as jnp
from jax import lax
from jax.sharding import PartitionSpec as P

FACTOR = 32
FEAT = 1024
damping_value = 0.1
HI = lax.Precision.HIGHEST


def local(query_grads, train_grads, token_counts, query_owner, module_map, out_basis, in_basis, eigen_values):
    slots = train_grads.shape[1]
    mine_q = query_grads.shape[0]
    first = lax.axis_index("mods") * slots
    module_ids = lax.dynamic_slice_in_dim(module_map, first, slots, 0)
    side_out = jnp.take(out_basis, module_ids, axis=0)
    side_in = jnp.take(in_basis, module_ids, axis=0)
    values = jnp.take(eigen_values, module_ids, axis=0).reshape(slots, FACTOR, FACTOR)
    half = side_in.astype(jnp.bfloat16).astype(jnp.float32)
    grads = query_grads.reshape(mine_q, slots, FACTOR, FACTOR)
    right = jnp.einsum("qsoi,sij->soqj", grads, side_in, precision=HI)
    both = jnp.einsum("sop,soqj->spqj", side_out, right, precision=HI)
    precond = (both / (values + damping_value)[:, :, None, :]).astype(jnp.bfloat16).astype(jnp.float32)
    back = jnp.einsum("sop,spqj->soqj", side_out, precond, precision=HI)
    back = jnp.einsum("soqj,sij->qsoi", back, half, precision=HI)
    back = back.astype(jnp.bfloat16).reshape(mine_q, slots * FEAT)
    full = lax.all_gather(back, "rows", axis=0, tiled=True)
    total = full.shape[0]
    hot = (jnp.arange(total, dtype=jnp.int32)[:, None] == query_owner[None, :]).astype(jnp.bfloat16)
    ordered = jnp.dot(hot, full, preferred_element_type=jnp.float32).astype(jnp.bfloat16)
    raw = lax.dot_general(
        ordered, train_grads.reshape(train_grads.shape[0], slots * FEAT), (((1,), (1,)), ((), ())),
        preferred_element_type=jnp.float32,
    )
    mine = lax.psum_scatter(raw, "mods", scatter_dimension=0, tiled=True)
    return mine / token_counts.astype(jnp.float32)[None, :]


def solution(mesh):
    in_specs = (
        P(("groups", "rows"), "mods", None),
        P(("groups", "rows"), "mods", None),
        P(("groups", "rows")),
        P("groups"),
        P(),
        P(),
        P(),
        P(),
    )
    out_specs = P(("groups", "mods"), "rows")
    return jax.shard_map(local, mesh=mesh, in_specs=in_specs, out_specs=out_specs, check_vma=False)
```

profile of v0, /device:TPU:0, one launch (start us, length us, event | category | flops | bytes accessed | tf_op | source)
XLA Modules:
  0.0 91.1 jit_solution(925511437159406929)
XLA Ops:
  6.5 0.0 copy-start
  6.5 0.0 copy-start.1
  6.5 0.0 all-gather.2.cloned.1.call-start
  6.5 0.8 compare_and_fusion
  7.3 1.8 %copy.10 = f32[64,4,1024]{0,2,1:T(8,128)S(1)} copy(f32[64,4,1024]{2,1,0:T(4,128)} %param.10) | data formatting | bytes 2097152 | tf_op args[0]
  9.1 0.0 copy-done
  9.1 0.6 gather_fusion.1
  9.7 0.0 copy-done.1
  9.7 0.6 gather_fusion
  10.2 0.1 gather.10
  10.3 0.1 copy.14
  10.4 1.5 %gather_fusion.2 = f32[4,32,32]{2,1,0:T(8,128)S(1)} fusion(f32[16,32,32]{2,1,0:T(8,128)} %param.15, s32[1024]{0:T(1024)S(1)} %pad_clamp_fusion), kind=kCustom, calls=%fused_computation.1.clone | custom fusion | bytes 32784 | tf_op jit(solution)/shard_map/jit(_take)/gather | solution.py:17
  11.9 0.1 select_add_fusion
  12.0 2.0 %convolution_bitcast_fusion = f32[4,32,64,32]{2,3,1,0:T(8,128)S(1)} fusion(f32[64,4,32,32]{0,3,2,1:T(8,128)S(1)} %bitcast.34, f32[4,32,32]{2,1,0:T(8,128)S(1)} %gather_fusion.1, pred[4]{0:T(512)(128)(4,1)S(1)} %get-tuple-element.6), kind=kOutput, calls=%fused_computation.9 | convolution fusion | flops 100667392 | bytes 2113540 | tf_op jit(solution)/shard_map/qsoi,sij->soqj/dot_general | solution.py:22
  14.0 3.2 %divide_convert_fusion = bf16[4,32,64,32]{2,1,3,0:T(8,128)(2,1)S(1)} fusion(f32[4,32,64,32]{2,3,1,0:T(8,128)S(1)} %convolution_bitcast_fusion, f32[4,32,32]{1,2,0:T(8,128)S(1)} %select_add_fusion, f32[4,32,32]{2,1,0:T(8,128)S(1)} %gather_fusion.2, pred[4]{0:T(512)(128)(4,1)S(1)} %get-tuple-element.6), kind=kOutput, calls=%fused_computation.8 | convolution fusion | flops 101191680 | bytes 1605636 | tf_op jit(solution)/shard_map/sop,soqj->spqj/dot_general | solution.py:23
  17.3 1.0 %fusion.14 = f32[4,32,64,32]{2,1,3,0:T(8,128)S(1)} fusion(bf16[4,32,64,32]{2,1,3,0:T(8,128)(2,1)S(1)} %divide_convert_fusion, f32[4,32,32]{2,1,0:T(8,128)S(1)} %gather_fusion.2, pred[4]{0:T(512)(128)(4,1)S(1)} %get-tuple-element.6), kind=kOutput, calls=%fused_computation.17 | convolution fusion | flops 100667392 | bytes 1589252 | tf_op jit(solution)/shard_map/sop,spqj->soqj/dot_general | solution.py:25
  18.3 2.5 %fusion.6 = bf16[4,32,32,64]{3,1,2,0:T(8,128)(2,1)S(1)} fusion(f32[4,32,64,32]{2,1,3,0:T(8,128)S(1)} %fusion.14, f32[4,32,32]{2,1,0:T(8,128)S(1)} %gather_fusion.1, pred[4]{0:T(512)(128)(4,1)S(1)} %get-tuple-element.6), kind=kOutput, calls=%fused_computation.10 | convolution fusion | flops 100929536 | bytes 1589252 | tf_op jit(solution)/shard_map/soqj,sij->qsoi/dot_general | solution.py:26
  20.8 1.2 %copy.16 = bf16[64,4096]{1,0:T(8,128)(2,1)} copy(bf16[64,4096]{0,1:T(8,128)(2,1)S(1)} %bitcast.35) | data formatting | bytes 1048576 | tf_op jit(solution)/shard_map/reshape | solution.py:27
  21.9 0.0 all-gather.2.cloned.1.call-update
  22.0 0.2 reduce-scatter.2.cloned.1.call-start
  22.2 0.0 copy-start.3
  22.2 12.1 %copy.25 = bf16[128,8,4,1024]{3,1,2,0:T(8,128)(2,1)} copy(bf16[128,8,4,1024]{3,2,1,0:T(4,128)(2,1)} %bitcast.32) | data formatting | bytes 16777216
  34.3 13.1 %all-gather.2.cloned.1.call-done = bf16[256,4096]{1,0:T(8,128)(2,1)} async-done(((bf16[64,4096]{1,0:T(8,128)(2,1)}), bf16[256,4096]{1,0:T(8,128)(2,1)}) %all-gather.2.cloned.1.call-update) | async-done | bytes 2097168 | tf_op jit(solution)/shard_map/all_gather | solution.py:28
  47.4 0.0 copy-done.3
  47.4 0.0 copy-start.2
  47.4 7.9 %fusion.9 = f32[256,1024]{1,0:T(8,128)} fusion(bf16[1024,4096]{1,0:T(8,128)(2,1)} %bitcast.33, bf16[256,4096]{1,0:T(8,128)(2,1)} %all-gather.2.cloned.1.call-done, s32[256]{0:T(256)S(1)} %copy-done.3), kind=kOutput, calls=%fused_computation.11 | convolution fusion | flops 2685468672 | bytes 11535360 | tf_op jit(solution)/shard_map/dot_general | solution.py:32
  55.3 0.0 reduce-scatter.2.cloned.1.call-update
  55.3 0.0 copy-done.2
  55.4 27.3 %reduce-scatter.2.cloned.1.call-done = f32[64,1024]{1,0:T(8,128)} async-done(((f32[256,1024]{1,0:T(8,128)}), f32[64,1024]{1,0:T(8,128)}) %reduce-scatter.2.cloned.1.call-update) | async-done | bytes 262160 | tf_op jit(solution)/shard_map/reduce_scatter | solution.py:36
  82.6 1.7 %broadcast_divide_fusion = f32[64,1024]{1,0:T(8,128)} fusion(f32[64,1024]{1,0:T(8,128)} %reduce-scatter.2.cloned.1.call-done, f32[1024]{0:T(1024)S(1)} %convert_element_type.26), kind=kLoop, calls=%fused_computation.13 | loop fusion | flops 65536 | bytes 528384 | tf_op jit(solution)/shard_map/div | solution.py:37
  (2 shorter events, 0.0 us)
Async XLA Ops:
  6.5 2.6 %copy-start = (f32[16,32,32]{2,1,0:T(8,128)S(1)}, f32[16,32,32]{2,1,0:T(8,128)}, u32[]{:S(2)}) copy-start(f32[16,32,32]{2,1,0:T(8,128)} %param.16) | copy-start | bytes 196612
  6.5 3.1 %copy-start.1 = (f32[16,1024]{1,0:T(8,128)S(1)}, f32[16,1024]{1,0:T(8,128)}, u32[]{:S(2)}) copy-start(f32[16,1024]{1,0:T(8,128)} %param.17) | copy-start | bytes 196612
  6.5 40.9 %all-gather.2.cloned.1.call-start = ((), (), s32[]{:S(2)}) async-start(), calls=%async_computation.1 | async-start | bytes 2621440 | tf_op jit(solution)/shard_map/all_gather | solution.py:28
  22.0 60.7 %reduce-scatter.2.cloned.1.call-start = ((), (), s32[]{:S(2)}) async-start(), calls=%async_computation.2 | async-start | bytes 1310720 | tf_op jit(solution)/shard_map/reduce_scatter | solution.py:36
  22.2 25.2 %copy-start.3 = (s32[256]{0:T(256)S(1)}, s32[256]{0:T(256)}, u32[]{:S(2)}) copy-start(s32[256]{0:T(256)} %param.13) | copy-start | bytes 3076
  47.4 7.9 %copy-start.2 = (s32[1024]{0:T(1024)S(1)}, s32[1024]{0:T(1024)}, u32[]{:S(2)}) copy-start(s32[1024]{0:T(1024)} %param.12) | copy-start | bytes 12292
Sparse Core Ops, SparseCore 0:
  22.1 25.2 all-gather.1
  55.5 27.1 reduce-scatter.1
where the time goes:
time: 91.4 us; the launch traced here: 91.1 us
  waiting for transfers between devices  40.4 us (44%)
  local copies, waits for them, and re-layouts  17.9 us (20%)
  matrix products  16.6 us (18%)
  between operations  13.5 us (15%)
  other arithmetic  2.54 us (3%)
    reduce_scatter x1, waiting for transfers between devices, local(): mine = lax.psum_scatter(raw, 'mods', scatter_dimension=0, tiled=True)  27.3 us
    unnamed x10, local copies, waits for them, and re-layouts  13.9 us
    all_gather x1, waiting for transfers between devices, local(): full = lax.all_gather(back, 'rows', axis=0, tiled=True)  13.1 us
    dot_general x1, matrix products, local(): lax.dot_general(ordered, train_grads.reshape(train_grads.shape[0], slots...  7.91 us
    dot_general x1, matrix products, local(): both = jnp.einsum('sop,soqj->spqj', side_out, right, precision=HI)  3.24 us
    dot_general x1, matrix products, local(): back = jnp.einsum('soqj,sij->qsoi', back, half, precision=HI)  2.46 us
    dot_general x1, matrix products, local(): right = jnp.einsum('qsoi,sij->soqj', grads, side_in, precision=HI)  2 us
  transfers between devices with their start and end apart: 2, of which 2 were waited for; matrix products, arithmetic and copies ran while one was open for 13% of the time, Pallas kernels for 0%

commit v1 on v0

v1 whole, which is shorter than its diff:
```python
import functools
import jax
import jax.numpy as jnp
from jax import lax
from jax.experimental import pallas as pl
from jax.experimental.pallas import tpu as pltpu
from jax.sharding import PartitionSpec as P

FACTOR = 32
FEAT = 1024
LANES = 128
TILE = 256
damping_value = 0.1
HI = lax.Precision.HIGHEST
MESH = pl.DeviceIdType.MESH


def kernel(
    rows, mods, back_ref, train_ref, owner_ref, counts_ref, out_ref,
    staged, train, full, raw, outgoing, incoming,
    train_sem, far_send, mate_send, gather_recv, sum_send, sum_recv,
):
    slots, mine_q, feat = back_ref.shape
    total_q = full.shape[1]
    train_rows = train.shape[1]
    tiles = train_rows // TILE
    block = out_ref.shape[0]
    columns = feat // LANES
    per_row = columns * slots
    chips = rows // 2
    me = lax.axis_index("rows")
    my_mod = lax.axis_index("mods")
    core = lax.rem(me, 2)
    mate = me + 1 - 2 * core
    fars = [lax.rem(me + 2 * hop, rows) for hop in range(1, chips)]
    others = [lax.rem(my_mod + hop, mods) for hop in range(1, mods)]

    barrier = pltpu.get_barrier_semaphore()
    for row in [mate] + fars:
        pl.semaphore_signal(barrier, inc=1, device_id={"rows": row}, device_id_type=MESH)
    for mod in others:
        pl.semaphore_signal(barrier, inc=1, device_id={"mods": mod}, device_id_type=MESH)

    segment = train_rows // slots
    loads = []
    for part in range(slots):
        span = pl.ds(part * segment * per_row, segment * per_row)
        load = pltpu.make_async_copy(train_ref.at[span], staged.at[span], train_sem.at[part])
        load.start()
        loads.append(load)

    def place(row):
        return pl.ds(pl.multiple_of(row * mine_q, mine_q), mine_q)

    for slot in range(slots):
        full[slot, place(me), :] = back_ref[slot]

    pl.semaphore_wait(barrier, 1 + len(fars) + len(others))

    def gather_copy(slot, owner, to, send):
        return pltpu.make_async_remote_copy(
            src_ref=full.at[slot, place(owner)],
            dst_ref=full.at[slot, place(owner)],
            send_sem=send,
            recv_sem=gather_recv.at[slot, owner],
            device_id={"rows": to},
            device_id_type=MESH,
        )

    sent = []
    for slot in range(slots):
        for hop, far in enumerate(fars):
            copy = gather_copy(slot, me, far, far_send.at[slot, hop])
            copy.start()
            sent.append(copy)
    for slot in range(slots):
        copy = gather_copy(slot, me, mate, mate_send.at[slot, 0])
        copy.start()
        sent.append(copy)

    size = 8 * per_row
    target = lax.broadcasted_iota(jnp.int32, (size, size), 0)
    source = lax.broadcasted_iota(jnp.int32, (size, size), 1)
    wanted = lax.rem(target, 8) * per_row + lax.rem(lax.div(target, 8), columns) * slots + lax.div(target, 8 * columns)
    sorter = (wanted == source).astype(jnp.float32).astype(jnp.bfloat16)

    def sort_segment(part):
        loads[part].wait()

        def step(i, carry):
            base = pl.multiple_of(i * 2 * size, 2 * size)
            first = jnp.dot(sorter, staged[pl.ds(base, size), :], preferred_element_type=jnp.float32)
            second = jnp.dot(sorter, staged[pl.ds(base + size, size), :], preferred_element_type=jnp.float32)
            where = pl.ds(pl.multiple_of(i * 16, 16), 16)
            for slot in range(slots):
                for column in range(columns):
                    at = (slot * columns + column) * 8
                    both = jnp.concatenate([first[at:at + 8], second[at:at + 8]], axis=0)
                    train[slot, where, column * LANES:(column + 1) * LANES] = both.astype(jnp.bfloat16)
            return carry

        steps = segment // 16
        lax.fori_loop(part * steps, (part + 1) * steps, step, 0)

    def forward(slot):
        for hop, far in enumerate(fars):
            gather_copy(slot, far, far, far_send.at[slot, hop]).wait_recv()
            copy = gather_copy(slot, far, mate, mate_send.at[slot, 1 + hop])
            copy.start()
            sent.append(copy)

    ids = lax.broadcasted_iota(jnp.int32, (total_q, total_q), 0)
    hot = (ids == owner_ref[...]).astype(jnp.float32).astype(jnp.bfloat16)

    def ordered(slot):
        gather_copy(slot, mate, mate, mate_send.at[slot, 0]).wait_recv()
        for far in fars:
            near = far + 1 - 2 * core
            gather_copy(slot, near, mate, mate_send.at[slot, 0]).wait_recv()
        return jnp.dot(hot, full[slot], preferred_element_type=jnp.float32).astype(jnp.bfloat16)

    def product(left, slot, tile):
        right = train[slot, tile * TILE:(tile + 1) * TILE, :]
        return lax.dot_general(left, right, (((1,), (1,)), ((), ())), preferred_element_type=jnp.float32)

    def accumulate(slot):
        left = ordered(slot)
        for tile in range(tiles):
            if slot == 0:
                raw[tile] = product(left, slot, tile)
            else:
                raw[tile] += product(left, slot, tile)

    def chunk(mod):
        return pl.ds(pl.multiple_of(mod * block, block), block)

    def sum_copy(tile, hop, to, landing):
        return pltpu.make_async_remote_copy(
            src_ref=outgoing.at[tile, chunk(to)],
            dst_ref=incoming.at[tile, landing],
            send_sem=sum_send.at[tile, hop],
            recv_sem=sum_recv.at[tile, landing],
            device_id={"mods": to},
            device_id_type=MESH,
        )

    half = slots // 2
    for part in range(half):
        sort_segment(part)
        forward(part)
    for part in range(half, slots):
        sort_segment(part)
    for slot in range(half):
        accumulate(slot)
    for slot in range(half, slots - 1):
        forward(slot)
        accumulate(slot)
    forward(slots - 1)
    left = ordered(slots - 1)
    for tile in range(tiles):
        done = raw[tile] + product(left, slots - 1, tile)
        raw[tile] = done
        outgoing[tile] = done.astype(jnp.bfloat16)
        for hop, mod in enumerate(others):
            copy = sum_copy(tile, hop, mod, mods - 2 - hop)
            copy.start()
            sent.append(copy)
    for tile in range(tiles):
        value = raw[tile, chunk(my_mod), :]
        for hop, mod in enumerate(others):
            sum_copy(tile, hop, mod, hop).wait_recv()
            value = value + incoming[tile, hop].astype(jnp.float32)
        where = slice(tile * TILE, (tile + 1) * TILE)
        out_ref[:, where] = value / counts_ref[:, where]
    for copy in sent:
        copy.wait_send()


def score(rows, mods, back, train_grads, owner, counts):
    slots, mine_q, feat = back.shape
    train_rows = train_grads.shape[0]
    columns = feat // LANES
    total_q = rows * mine_q
    tiles = train_rows // TILE
    block = total_q // mods
    staged = train_grads.reshape(train_rows, slots, columns, LANES).transpose(0, 2, 1, 3).reshape(-1, LANES)
    vmem = pl.BlockSpec(memory_space=pltpu.VMEM)
    chips = rows // 2
    return pl.pallas_call(
        functools.partial(kernel, rows, mods),
        out_shape=jax.ShapeDtypeStruct((block, train_rows), jnp.float32),
        in_specs=[vmem, pl.BlockSpec(memory_space=pl.ANY), vmem, vmem],
        out_specs=vmem,
        scratch_shapes=[
            pltpu.VMEM(staged.shape, jnp.bfloat16),
            pltpu.VMEM((slots, train_rows, feat), jnp.bfloat16),
            pltpu.VMEM((slots, total_q, feat), jnp.bfloat16),
            pltpu.VMEM((tiles, total_q, TILE), jnp.float32),
            pltpu.VMEM((tiles, total_q, TILE), jnp.bfloat16),
            pltpu.VMEM((tiles, mods - 1, block, TILE), jnp.bfloat16),
            pltpu.SemaphoreType.DMA((slots,)),
            pltpu.SemaphoreType.DMA((slots, max(chips - 1, 1))),
            pltpu.SemaphoreType.DMA((slots, chips)),
            pltpu.SemaphoreType.DMA((slots, rows)),
            pltpu.SemaphoreType.DMA((tiles, mods - 1)),
            pltpu.SemaphoreType.DMA((tiles, mods - 1)),
        ],
        compiler_params=pltpu.CompilerParams(
            collective_id=0, has_side_effects=True, vmem_limit_bytes=56 * 1024 * 1024
        ),
        name="score",
    )(back, staged, owner, counts)


def local(rows, mods, query_grads, train_grads, token_counts, query_owner, module_map, out_basis, in_basis, eigen_values):
    slots = train_grads.shape[1]
    mine_q = query_grads.shape[0]
    first = lax.axis_index("mods") * slots
    module_ids = lax.dynamic_slice_in_dim(module_map, first, slots, 0)
    side_out = jnp.take(out_basis, module_ids, axis=0)
    side_in = jnp.take(in_basis, module_ids, axis=0)
    values = jnp.take(eigen_values, module_ids, axis=0).reshape(slots, FACTOR, FACTOR)
    half = side_in.astype(jnp.bfloat16).astype(jnp.float32)
    grads = query_grads.reshape(mine_q, slots, FACTOR, FACTOR)
    right = jnp.einsum("qsoi,sij->soqj", grads, side_in, precision=HI)
    both = jnp.einsum("sop,soqj->spqj", side_out, right, precision=HI)
    precond = (both / (values + damping_value)[:, :, None, :]).astype(jnp.bfloat16).astype(jnp.float32)
    back = jnp.einsum("sop,spqj->soqj", side_out, precond, precision=HI)
    back = jnp.einsum("soqj,sij->sqoi", back, half, precision=HI)
    back = back.astype(jnp.bfloat16).reshape(slots, mine_q, FEAT)
    return score(rows, mods, back, train_grads, query_owner[None, :], token_counts.astype(jnp.float32)[None, :])


def solution(mesh):
    in_specs = (
        P(("groups", "rows"), "mods", None),
        P(("groups", "rows"), "mods", None),
        P(("groups", "rows")),
        P("groups"),
        P(),
        P(),
        P(),
        P(),
    )
    out_specs = P(("groups", "mods"), "rows")
    body = functools.partial(local, mesh.shape["rows"], mesh.shape["mods"])
    return jax.shard_map(body, mesh=mesh, in_specs=in_specs, out_specs=out_specs, check_vma=False)
```

time: 91.4 us -> 61.1 us (0.67)
  waiting for transfers between devices: 40.4 us -> 0 us
  Pallas kernels: 0 us -> 40.2 us
  between operations: 13.5 us -> 0.09 us
  local copies, waits for them, and re-layouts: 17.9 us -> 7.54 us
  matrix products: 16.6 us -> 11.6 us
  other arithmetic: 2.54 us -> 1.45 us
    pallas_call x0 -> x1, Pallas kernels: none -> 40.2 us  [score(): pl.pallas_call(functools.partial(kernel, rows, mods), out_shape=jax.Shape...]
    reduce_scatter x1 -> x0, waiting for transfers between devices: 27.3 us -> none  [local(): mine = lax.psum_scatter(raw, 'mods', scatter_dimension=0, tiled=True)]
    all_gather x1 -> x0, waiting for transfers between devices: 13.1 us -> none  [local(): full = lax.all_gather(back, 'rows', axis=0, tiled=True)]
    unnamed x10 -> x8, local copies, waits for them, and re-layouts: 13.9 us -> 3.63 us
    dot_general x2 -> x1, matrix products: 10.4 us -> 2.46 us  [local(): back = jnp.einsum('soqj,sij->sqoi', back, half, precision=HI)]
    div x1 -> x0, other arithmetic: 1.68 us -> none  [local(): return mine / token_counts.astype(jnp.float32)[None, :]]
    dot_general x1, matrix products: 3.24 us -> 4.77 us  [local(): both = jnp.einsum('sop,soqj->spqj', side_out, right, precision=HI)]
    dot_general x1, matrix products: 2 us -> 3.31 us  [local(): right = jnp.einsum('qsoi,sij->soqj', grads, side_in, precision=HI)]
  transfers between devices with their start and end apart: 2 -> 0, of which waited for: 2 -> 0; matrix products, arithmetic and copies ran while one was open for 13% -> 0% of each run, Pallas kernels for 0% -> 0%
where the time goes in v1:
time: 61.1 us; the launch traced here: 60.8 us
  Pallas kernels  40.2 us (66%)
  matrix products  11.6 us (19%)
  local copies, waits for them, and re-layouts  7.54 us (12%)
  other arithmetic  1.45 us (2%)
    pallas_call x1, Pallas kernels, score(): pl.pallas_call(functools.partial(kernel, rows, mods), out_shape=jax.Shape...  40.2 us
    dot_general x1, matrix products, local(): both = jnp.einsum('sop,soqj->spqj', side_out, right, precision=HI)  4.77 us
    unnamed x8, local copies, waits for them, and re-layouts  3.63 us
    dot_general x1, matrix products, local(): right = jnp.einsum('qsoi,sij->soqj', grads, side_in, precision=HI)  3.31 us
    dot_general x1, matrix products, local(): back = jnp.einsum('soqj,sij->sqoi', back, half, precision=HI)  2.46 us
    gather x1, local copies, waits for them, and re-layouts, local(): side_out = jnp.take(out_basis, module_ids, axis=0)  1.5 us

profile of v1, /device:TPU:0, one launch (start us, length us, event | category | flops | bytes accessed | tf_op | source)
XLA Modules:
  0.0 60.8 jit_solution(16735191553553159776)
XLA Ops:
  0.0 0.0 copy-start
  0.0 0.8 %compare_and_fusion = (pred[4]{0:T(512)(128)(4,1)S(1)}, s32[4]{0:T(128)S(1)}) fusion(s32[16]{0:T(128)} %param.14, s32[]{:T(128)S(6)} %select_n.23), kind=kLoop, calls=%fused_computation.30 | loop fusion | flops 24 | bytes 40 | tf_op jit(solution)/shard_map/jit(_take)/and | solution.py:221
  0.8 0.2 copy-done
  1.0 0.6 gather_fusion.1
  1.5 1.8 %copy.14 = f32[64,4,1024]{0,2,1:T(8,128)S(1)} copy(f32[64,4,1024]{2,1,0:T(4,128)} %param.10) | data formatting | bytes 2097152 | tf_op args[0]
  3.3 0.0 copy-start.1
  3.3 3.3 %convolution_bitcast_fusion = f32[4,32,64,32]{2,3,1,0:T(8,128)} fusion(f32[64,4,32,32]{0,3,2,1:T(8,128)S(1)} %bitcast.36, f32[4,32,32]{2,1,0:T(8,128)S(1)} %gather_fusion.1, pred[4]{0:T(512)(128)(4,1)S(1)} %get-tuple-element.6), kind=kOutput, calls=%fused_computation.8 | convolution fusion | flops 100667392 | bytes 2113540 | tf_op jit(solution)/shard_map/qsoi,sij->soqj/dot_general | solution.py:225
  6.6 0.0 copy-done.1
  6.6 0.6 gather_fusion
  7.2 0.1 gather.10
  7.3 0.1 copy.18
  7.4 0.1 select_add_fusion
  7.4 1.5 %gather_fusion.2 = f32[4,32,32]{2,1,0:T(8,128)S(1)} fusion(f32[16,32,32]{2,1,0:T(8,128)} %param.15, s32[1024]{0:T(1024)S(1)} %pad_clamp_fusion), kind=kCustom, calls=%fused_computation.1.clone | custom fusion | bytes 32784 | tf_op jit(solution)/shard_map/jit(_take)/gather | solution.py:220
  8.9 4.8 %divide_convert_fusion = bf16[4,32,64,32]{2,1,3,0:T(8,128)(2,1)S(1)} fusion(f32[4,32,64,32]{2,3,1,0:T(8,128)} %convolution_bitcast_fusion, f32[4,32,32]{1,2,0:T(8,128)S(1)} %select_add_fusion, f32[4,32,32]{2,1,0:T(8,128)S(1)} %gather_fusion.2, pred[4]{0:T(512)(128)(4,1)S(1)} %get-tuple-element.6), kind=kOutput, calls=%fused_computation.7 | convolution fusion | flops 101191680 | bytes 1605636 | tf_op jit(solution)/shard_map/sop,soqj->spqj/dot_general | solution.py:226
  13.7 1.0 %fusion.11 = f32[4,32,64,32]{2,1,3,0:T(8,128)S(1)} fusion(bf16[4,32,64,32]{2,1,3,0:T(8,128)(2,1)S(1)} %divide_convert_fusion, f32[4,32,32]{2,1,0:T(8,128)S(1)} %gather_fusion.2, pred[4]{0:T(512)(128)(4,1)S(1)} %get-tuple-element.6), kind=kOutput, calls=%fused_computation.12 | convolution fusion | flops 100667392 | bytes 1589252 | tf_op jit(solution)/shard_map/sop,spqj->soqj/dot_general | solution.py:228
  14.8 0.0 copy-start.2
  14.8 2.5 %fusion.6 = bf16[4,32,32,64]{3,1,2,0:T(8,128)(2,1)S(1)} fusion(f32[4,32,64,32]{2,1,3,0:T(8,128)S(1)} %fusion.11, f32[4,32,32]{2,1,0:T(8,128)S(1)} %gather_fusion.1, pred[4]{0:T(512)(128)(4,1)S(1)} %get-tuple-element.6), kind=kOutput, calls=%fused_computation.9 | convolution fusion | flops 100929536 | bytes 1589252 | tf_op jit(solution)/shard_map/soqj,sij->sqoi/dot_general | solution.py:229
  17.3 1.1 %copy.21.back_ref = bf16[4,64,1024]{2,1,0:T(8,128)(2,1)} copy(bf16[4,64,1024]{1,2,0:T(8,128)(2,1)S(1)} %bitcast.37) | data formatting | bytes 1048576 | tf_op jit(solution)/shard_map/reshape | solution.py:230
  18.4 0.0 copy-done.2
  18.4 0.6 convert_element_type.21
  19.0 40.2 %score.1 = f32[64,1024]{1,0:T(8,128)} custom-call(bf16[4,64,1024]{2,1,0:T(8,128)(2,1)} %copy.21.back_ref, bf16[32768,128]{1,0:T(8,128)(2,1)} %bitcast.35, s32[1,256]{1,0:T(1,128)} %bitcast.39, f32[1,1024]{1,0:T(1,128)} %bitcast.38), custom_call_target="tpu_custom_call" | custom-call | tf_op jit(solution)/shard_map/score/pallas_call | solution.py:189
  59.2 1.7 %copy.39 = f32[64,1024]{1,0:T(8,128)} copy(f32[64,1024]{1,0:T(8,128)} %score.1) | data formatting | bytes 524288
  (1 shorter events, 0.0 us)
Async XLA Ops:
  0.0 1.0 %copy-start = (f32[16,32,32]{2,1,0:T(8,128)S(1)}, f32[16,32,32]{2,1,0:T(8,128)}, u32[]{:S(2)}) copy-start(f32[16,32,32]{2,1,0:T(8,128)} %param.16) | copy-start | bytes 196612
  3.3 3.3 %copy-start.1 = (f32[16,1024]{1,0:T(8,128)S(1)}, f32[16,1024]{1,0:T(8,128)}, u32[]{:S(2)}) copy-start(f32[16,1024]{1,0:T(8,128)} %param.17) | copy-start | bytes 196612
  14.8 3.6 %copy-start.2 = (s32[1024]{0:T(1024)S(1)}, s32[1024]{0:T(1024)}, u32[]{:S(2)}) copy-start(s32[1024]{0:T(1024)} %param.12) | copy-start | bytes 12292

commit v2 on v1

--- a/solution.py
+++ b/solution.py
@@ -11,18 +11,125 @@
 LANES = 128
 TILE = 256
 damping_value = 0.1
-HI = lax.Precision.HIGHEST
 MESH = pl.DeviceIdType.MESH
 
 
+def split(value):
+    high = value.astype(jnp.bfloat16)
+    return high, (value - high.astype(jnp.float32)).astype(jnp.bfloat16)
+
+
+def mask(value):
+    return value.astype(jnp.float32).astype(jnp.bfloat16)
+
+
+def rotate(
+    slots, my_mod, query_ref, map_ref, out_basis_ref, in_basis_ref, eigen_ref,
+    spread, right_ref, precond_ref, back_ref, damped, full, place,
+):
+    mine_q = right_ref.shape[1]
+    columns = FEAT // LANES
+    group = LANES // FACTOR
+    wide = group * LANES
+    modules = [map_ref[my_mod * slots + slot] for slot in range(slots)]
+    iota = lambda shape, axis: lax.broadcasted_iota(jnp.int32, shape, axis)
+    dot = functools.partial(jnp.dot, preferred_element_type=jnp.float32)
+
+    repeat = mask(iota((FACTOR, wide), 0) == lax.rem(iota((FACTOR, wide), 1), FACTOR))
+    lane = iota((LANES, wide), 1)
+    same_row = lax.div(iota((LANES, wide), 0), FACTOR) == lax.div(lane, LANES)
+    highs, lows = [], []
+    for slot in range(slots):
+        side_in = in_basis_ref[modules[slot]]
+        keep = same_row & (lax.div(lax.rem(lane, LANES), FACTOR) == slot)
+        for value, parts in zip(split(jnp.concatenate([side_in] * group, axis=0)), (highs, lows)):
+            parts.append(jnp.where(keep, dot(value, repeat), 0.0).astype(jnp.bfloat16))
+    block_high = jnp.concatenate(highs, axis=0)
+    block_low = jnp.concatenate(lows, axis=0)
+
+    shape = (slots * FACTOR, FACTOR * LANES)
+    row, lane = iota(shape, 0), iota(shape, 1)
+    pick = mask(
+        (lax.rem(row, FACTOR) == lax.div(lane, LANES))
+        & (lax.div(row, FACTOR) == lax.div(lax.rem(lane, LANES), FACTOR))
+    )
+    sides = jnp.concatenate([out_basis_ref[modules[slot]] for slot in range(slots)], axis=0)
+    over = lambda left: lax.dot_general(left, pick, (((0,), (0,)), ((), ())), preferred_element_type=jnp.float32)
+    high = sides.astype(jnp.bfloat16)
+    rest = sides - high.astype(jnp.float32)
+    middle, low = split(rest)
+    spread_all = over(high) + (over(middle) + over(low))
+    for o in range(FACTOR):
+        spread[o] = spread_all[:, o * LANES:(o + 1) * LANES]
+
+    shape = (FACTOR, FEAT)
+    own = lax.div(iota(shape, 1), FACTOR) == iota(shape, 0)
+    fold = mask(lax.rem(iota((FEAT, LANES), 0), FACTOR) == lax.rem(iota((FEAT, LANES), 1), FACTOR))
+    slot_of = lax.div(iota((FACTOR, LANES), 1), FACTOR)
+    values = jnp.zeros((FACTOR, LANES), jnp.float32)
+    for slot in range(slots):
+        rows = jnp.where(own, eigen_ref[pl.ds(modules[slot], 1), :], 0.0)
+        high = rows.astype(jnp.bfloat16)
+        middle, low = split(rows - high.astype(jnp.float32))
+        values = jnp.where(slot_of == slot, dot(high, fold) + (dot(middle, fold) + dot(low, fold)), values)
+    damped[...] = values + damping_value
+
+    for column in range(columns):
+        grads = jnp.concatenate(
+            [query_ref[pl.ds(column * slots + slot, mine_q, stride=columns * slots), :] for slot in range(slots)], axis=1
+        )
+        high, low = split(grads)
+        right = dot(high, block_high) + (dot(low, block_high) + dot(high, block_low))
+        for o in range(group):
+            right_ref[column * group + o] = right[:, o * LANES:(o + 1) * LANES]
+
+    def forth(pair, carry):
+        p = pair * 2
+        sums = [jnp.zeros((mine_q, LANES), jnp.float32) for _ in range(2)]
+        for o in range(FACTOR):
+            right = right_ref[o]
+            for k in range(2):
+                sums[k] = sums[k] + right * spread[o, pl.ds(p + k, 1), :]
+        for k in range(2):
+            value = sums[k] / damped[pl.ds(p + k, 1), :]
+            precond_ref[p + k] = value.astype(jnp.bfloat16).astype(jnp.float32)
+        return carry
+
+    lax.fori_loop(0, FACTOR // 2, forth, 0)
+
+    def back(pair, carry):
+        o = pair * 2
+        sums = [jnp.zeros((mine_q, LANES), jnp.float32) for _ in range(2)]
+        for p in range(FACTOR):
+            value = precond_ref[p]
+            for k in range(2):
+                sums[k] = sums[k] + value * spread[o + k, p:p + 1, :]
+        for k in range(2):
+            back_ref[o + k] = sums[k]
+        return carry
+
+    lax.fori_loop(0, FACTOR // 2, back, 0)
+
+    turn = lambda left: lax.dot_general(
+        left, block_high, (((1,), (1,)), ((), ())), preferred_element_type=jnp.float32
+    )
+    for column in range(columns):
+        value = jnp.concatenate([back_ref[column * group + o] for o in range(group)], axis=1)
+        high, low = split(value)
+        result = (turn(high) + turn(low)).astype(jnp.bfloat16)
+        for slot in range(slots):
+            full[slot, place, column * LANES:(column + 1) * LANES] = result[:, slot * LANES:(slot + 1) * LANES]
+
+
 def kernel(
-    rows, mods, back_ref, train_ref, owner_ref, counts_ref, out_ref,
+    rows, mods, query_ref, train_ref, owner_ref, counts_ref, map_ref, out_basis_ref, in_basis_ref, eigen_ref, out_ref,
+    spread, right_ref, precond_ref, back_ref, damped,
     staged, train, full, raw, outgoing, incoming,
     train_sem, far_send, mate_send, gather_recv, sum_send, sum_recv,
 ):
-    slots, mine_q, feat = back_ref.shape
+    slots, train_rows, feat = train.shape
+    mine_q = right_ref.shape[1]
     total_q = full.shape[1]
-    train_rows = train.shape[1]
     tiles = train_rows // TILE
     block = out_ref.shape[0]
     columns = feat // LANES
@@ -52,8 +159,10 @@
     def place(row):
         return pl.ds(pl.multiple_of(row * mine_q, mine_q), mine_q)
 
-    for slot in range(slots):
-        full[slot, place(me), :] = back_ref[slot]
+    rotate(
+        slots, my_mod, query_ref, map_ref, out_basis_ref, in_basis_ref, eigen_ref,
+        spread, right_ref, precond_ref, back_ref, damped, full, place(me),
+    )
 
     pl.semaphore_wait(barrier, 1 + len(fars) + len(others))
 
@@ -171,27 +280,35 @@
             sum_copy(tile, hop, mod, hop).wait_recv()
             value = value + incoming[tile, hop].astype(jnp.float32)
         where = slice(tile * TILE, (tile + 1) * TILE)
-        out_ref[:, where] = value / counts_ref[:, where]
+        out_ref[:, where] = value / counts_ref[:, where].astype(jnp.float32)
     for copy in sent:
         copy.wait_send()
 
 
-def score(rows, mods, back, train_grads, owner, counts):
-    slots, mine_q, feat = back.shape
-    train_rows = train_grads.shape[0]
+def local(rows, mods, query_grads, train_grads, token_counts, query_owner, module_map, out_basis, in_basis, eigen_values):
+    mine_q = query_grads.shape[0]
+    train_rows, slots, feat = train_grads.shape
     columns = feat // LANES
     total_q = rows * mine_q
     tiles = train_rows // TILE
     block = total_q // mods
     staged = train_grads.reshape(train_rows, slots, columns, LANES).transpose(0, 2, 1, 3).reshape(-1, LANES)
+    queries = query_grads.reshape(mine_q, slots, columns, LANES).transpose(0, 2, 1, 3).reshape(-1, LANES)
+    owner = query_owner[None, :]
+    counts = token_counts[None, :]
     vmem = pl.BlockSpec(memory_space=pltpu.VMEM)
     chips = rows // 2
     return pl.pallas_call(
         functools.partial(kernel, rows, mods),
         out_shape=jax.ShapeDtypeStruct((block, train_rows), jnp.float32),
-        in_specs=[vmem, pl.BlockSpec(memory_space=pl.ANY), vmem, vmem],
+        in_specs=[vmem, pl.BlockSpec(memory_space=pl.ANY), vmem, vmem, pl.BlockSpec(memory_space=pltpu.SMEM), vmem, vmem, vmem],
         out_specs=vmem,
         scratch_shapes=[
+            pltpu.VMEM((FACTOR, FACTOR, LANES), jnp.float32),
+            pltpu.VMEM((FACTOR, mine_q, LANES), jnp.float32),
+            pltpu.VMEM((FACTOR, mine_q, LANES), jnp.float32),
+            pltpu.VMEM((FACTOR, mine_q, LANES), jnp.float32),
+            pltpu.VMEM((FACTOR, LANES), jnp.float32),
             pltpu.VMEM(staged.shape, jnp.bfloat16),
             pltpu.VMEM((slots, train_rows, feat), jnp.bfloat16),
             pltpu.VMEM((slots, total_q, feat), jnp.bfloat16),
@@ -209,26 +326,7 @@
             collective_id=0, has_side_effects=True, vmem_limit_bytes=56 * 1024 * 1024
         ),
         name="score",
-    )(back, staged, owner, counts)
-
-
-def local(rows, mods, query_grads, train_grads, token_counts, query_owner, module_map, out_basis, in_basis, eigen_values):
-    slots = train_grads.shape[1]
-    mine_q = query_grads.shape[0]
-    first = lax.axis_index("mods") * slots
-    module_ids = lax.dynamic_slice_in_dim(module_map, first, slots, 0)
-    side_out = jnp.take(out_basis, module_ids, axis=0)
-    side_in = jnp.take(in_basis, module_ids, axis=0)
-    values = jnp.take(eigen_values, module_ids, axis=0).reshape(slots, FACTOR, FACTOR)
-    half = side_in.astype(jnp.bfloat16).astype(jnp.float32)
-    grads = query_grads.reshape(mine_q, slots, FACTOR, FACTOR)
-    right = jnp.einsum("qsoi,sij->soqj", grads, side_in, precision=HI)
-    both = jnp.einsum("sop,soqj->spqj", side_out, right, precision=HI)
-    precond = (both / (values + damping_value)[:, :, None, :]).astype(jnp.bfloat16).astype(jnp.float32)
-    back = jnp.einsum("sop,spqj->soqj", side_out, precond, precision=HI)
-    back = jnp.einsum("soqj,sij->sqoi", back, half, precision=HI)
-    back = back.astype(jnp.bfloat16).reshape(slots, mine_q, FEAT)
-    return score(rows, mods, back, train_grads, query_owner[None, :], token_counts.astype(jnp.float32)[None, :])
+    )(queries, staged, owner, counts, module_map, out_basis, in_basis, eigen_values)
 
 
 def solution(mesh):

time: 61.1 us -> 51.6 us (0.84)
  matrix products: 11.6 us -> 0 us
  Pallas kernels: 40.2 us -> 49.8 us
  local copies, waits for them, and re-layouts: 7.54 us -> 1.67 us
  other arithmetic: 1.45 us -> 0 us
    dot_general x4 -> x0, matrix products: 11.6 us -> none  [the longest x1 4.77 us: local(): both = jnp.einsum('sop,soqj->spqj', side_out, right, precision=HI)]
    pallas_call x1, Pallas kernels: 40.2 us -> 49.8 us  [local(): pl.pallas_call(functools.partial(kernel, rows, mods), out_shape=jax.Shape...]
    gather x5 -> x0, local copies, waits for them, and re-layouts: 2.79 us -> none  [the longest x1 1.5 us: local(): side_out = jnp.take(out_basis, module_ids, axis=0)]
    unnamed x8 -> x1, local copies, waits for them, and re-layouts: 3.63 us -> 1.67 us
    reshape x1 -> x0, local copies, waits for them, and re-layouts: 1.12 us -> none  [local(): back = back.astype(jnp.bfloat16).reshape(slots, mine_q, FEAT)]
    and x1 -> x0, other arithmetic: 0.78 us -> none  [local(): side_in = jnp.take(in_basis, module_ids, axis=0)]
where the time goes in v2:
time: 51.6 us; the launch traced here: 51.5 us
  Pallas kernels  49.8 us (97%)
  local copies, waits for them, and re-layouts  1.67 us (3%)
    pallas_call x1, Pallas kernels, local(): pl.pallas_call(functools.partial(kernel, rows, mods), out_shape=jax.Shape...  49.8 us
    unnamed x1, local copies, waits for them, and re-layouts  1.67 us

profile of v2, /device:TPU:0, one launch (start us, length us, event | category | flops | bytes accessed | tf_op | source)
XLA Modules:
  0.0 51.5 jit_solution(12402442303818434301)
XLA Ops:
  0.0 49.8 %score.1 = f32[64,1024]{1,0:T(8,128)} custom-call(f32[2048,128]{1,0:T(8,128)} %bitcast.13, bf16[32768,128]{1,0:T(8,128)(2,1)} %bitcast.12, s32[1,256]{1,0:T(1,128)} %bitcast.15, s32[1,1024]{1,0:T(1,128)} %bitcast.14, s32[16]{0:T(128)} %map_ref.1, f32[16,32,32]{2,1,0:T(8,128)} %out_basis_ref.1, f32[16,32,32]{2,1,0:T(8,128)} %in_basis_ref.1, f32[16,1024]{1,0:T(8,128)} %eigen_ref.1), custom_call_target="tpu_custom_call" | custom-call | tf_op jit(solution)/shard_map/score/pallas_call | solution.py:301
  49.8 1.7 %copy.12 = f32[64,1024]{1,0:T(8,128)} copy(f32[64,1024]{1,0:T(8,128)} %score.1) | data formatting | bytes 524288

commit v3 on v2

v3 whole, which is shorter than its diff:
```python
import functools
import jax
import jax.numpy as jnp
from jax import lax
from jax.experimental import pallas as pl
from jax.experimental.pallas import tpu as pltpu
from jax.sharding import PartitionSpec as P

FACTOR = 32
FEAT = 1024
LANES = 128
FACTOR_BITS = 5
LANE_BITS = 7
HALVES = 2
TILE = 256
damping_value = 0.1
MESH = pl.DeviceIdType.MESH


def split(value):
    high = value.astype(jnp.bfloat16)
    return high, (value - high.astype(jnp.float32)).astype(jnp.bfloat16)


def mask(value):
    return value.astype(jnp.float32).astype(jnp.bfloat16)


def rotate(
    slots, my_mod, query_ref, map_ref, out_basis_ref, in_basis_ref, eigen_ref,
    spread, right_ref, precond_ref, back_ref, damped, full, place,
):
    mine_q = right_ref.shape[1] * HALVES
    columns = FEAT // LANES
    group = LANES // FACTOR
    wide = group * LANES
    modules = [map_ref[my_mod * slots + slot] for slot in range(slots)]
    iota = lambda shape, axis: lax.broadcasted_iota(jnp.int32, shape, axis)
    dot = functools.partial(jnp.dot, preferred_element_type=jnp.float32)

    repeat = mask(iota((FACTOR, wide), 0) == (iota((FACTOR, wide), 1) & (FACTOR - 1)))
    lane = iota((LANES, wide), 1)
    same_row = (iota((LANES, wide), 0) >> FACTOR_BITS) == (lane >> LANE_BITS)
    highs, lows = [], []
    for slot in range(slots):
        side_in = in_basis_ref[modules[slot]]
        keep = same_row & (((lane & (LANES - 1)) >> FACTOR_BITS) == slot)
        for value, parts in zip(split(jnp.concatenate([side_in] * group, axis=0)), (highs, lows)):
            parts.append(jnp.where(keep, dot(value, repeat), 0.0).astype(jnp.bfloat16))
    block_high = jnp.concatenate(highs, axis=0)
    block_low = jnp.concatenate(lows, axis=0)

    shape = (slots * FACTOR, FACTOR * LANES)
    row, lane = iota(shape, 0), iota(shape, 1)
    pick = mask(
        ((row & (FACTOR - 1)) == (lane >> LANE_BITS))
        & ((row >> FACTOR_BITS) == ((lane & (LANES - 1)) >> FACTOR_BITS))
    )
    sides = jnp.concatenate([out_basis_ref[modules[slot]] for slot in range(slots)], axis=0)
    over = lambda left: lax.dot_general(left, pick, (((0,), (0,)), ((), ())), preferred_element_type=jnp.float32)
    high = sides.astype(jnp.bfloat16)
    rest = sides - high.astype(jnp.float32)
    middle, low = split(rest)
    spread_all = over(high) + (over(middle) + over(low))
    for o in range(FACTOR):
        spread[o] = spread_all[:, o * LANES:(o + 1) * LANES]

    shape = (FACTOR, FEAT)
    own = (iota(shape, 1) >> FACTOR_BITS) == iota(shape, 0)
    fold = mask((iota((FEAT, LANES), 0) & (FACTOR - 1)) == (iota((FEAT, LANES), 1) & (FACTOR - 1)))
    slot_of = iota((FACTOR, LANES), 1) >> FACTOR_BITS
    values = jnp.zeros((FACTOR, LANES), jnp.float32)
    for slot in range(slots):
        rows = jnp.where(own, eigen_ref[pl.ds(modules[slot], 1), :], 0.0)
        high = rows.astype(jnp.bfloat16)
        middle, low = split(rows - high.astype(jnp.float32))
        values = jnp.where(slot_of == slot, dot(high, fold) + (dot(middle, fold) + dot(low, fold)), values)
    damped[...] = values + damping_value

    turn = lambda left: lax.dot_general(
        left, block_high, (((1,), (1,)), ((), ())), preferred_element_type=jnp.float32
    )
    count = mine_q // HALVES
    together = 4

    def run(half):
        start = half * count
        for column in range(columns):
            grads = jnp.concatenate(
                [
                    query_ref[pl.ds((start * columns + column) * slots + slot, count, stride=columns * slots), :]
                    for slot in range(slots)
                ],
                axis=1,
            )
            high, low = split(grads)
            right = dot(high, block_high) + (dot(low, block_high) + dot(high, block_low))
            for o in range(group):
                right_ref[column * group + o] = right[:, o * LANES:(o + 1) * LANES]

        def forth(step, carry):
            p = step * together
            sums = [jnp.zeros((count, LANES), jnp.float32) for _ in range(together)]
            for o in range(FACTOR):
                right = right_ref[o]
                for k in range(together):
                    sums[k] = sums[k] + right * spread[o, pl.ds(p + k, 1), :]
            for k in range(together):
                value = sums[k] / damped[pl.ds(p + k, 1), :]
                precond_ref[p + k] = value.astype(jnp.bfloat16).astype(jnp.float32)
            return carry

        lax.fori_loop(0, FACTOR // together, forth, 0)

        def back(step, carry):
            o = step * together
            sums = [jnp.zeros((count, LANES), jnp.float32) for _ in range(together)]
            for p in range(FACTOR):
                value = precond_ref[p]
                for k in range(together):
                    sums[k] = sums[k] + value * spread[o + k, p:p + 1, :]
            for k in range(together):
                back_ref[o + k] = sums[k]
            return carry

        lax.fori_loop(0, FACTOR // together, back, 0)

        for column in range(columns):
            value = jnp.concatenate([back_ref[column * group + o] for o in range(group)], axis=1)
            high, low = split(value)
            result = (turn(high) + turn(low)).astype(jnp.bfloat16)
            for slot in range(slots):
                full[slot, place(half), column * LANES:(column + 1) * LANES] = result[:, slot * LANES:(slot + 1) * LANES]

    return run


def kernel(
    rows, mods, query_ref, train_ref, owner_ref, counts_ref, map_ref, out_basis_ref, in_basis_ref, eigen_ref, out_ref,
    spread, right_ref, precond_ref, back_ref, damped,
    staged, train, full, raw, outgoing, incoming,
    train_sem, far_send, mate_send, gather_recv, sum_send, sum_recv,
):
    slots, train_rows, feat = train.shape
    mine_q = right_ref.shape[1] * HALVES
    total_q = full.shape[1]
    tiles = train_rows // TILE
    block = out_ref.shape[0]
    columns = feat // LANES
    per_row = columns * slots
    chips = rows // 2
    me = lax.axis_index("rows")
    my_mod = lax.axis_index("mods")
    core = lax.rem(me, 2)
    mate = me + 1 - 2 * core
    fars = [lax.rem(me + 2 * hop, rows) for hop in range(1, chips)]
    others = [lax.rem(my_mod + hop, mods) for hop in range(1, mods)]

    barrier = pltpu.get_barrier_semaphore()
    for row in [mate] + fars:
        pl.semaphore_signal(barrier, inc=1, device_id={"rows": row}, device_id_type=MESH)
    for mod in others:
        pl.semaphore_signal(barrier, inc=1, device_id={"mods": mod}, device_id_type=MESH)

    segment = train_rows // slots
    loads = []
    for part in range(slots):
        span = pl.ds(part * segment * per_row, segment * per_row)
        load = pltpu.make_async_copy(train_ref.at[span], staged.at[span], train_sem.at[part])
        load.start()
        loads.append(load)

    count = mine_q // HALVES

    def place(row, half):
        return pl.ds(pl.multiple_of(row * mine_q + half * count, count), count)

    def gather_copy(half, slot, owner, to, send):
        return pltpu.make_async_remote_copy(
            src_ref=full.at[slot, place(owner, half)],
            dst_ref=full.at[slot, place(owner, half)],
            send_sem=send,
            recv_sem=gather_recv.at[half, slot, owner],
            device_id={"rows": to},
            device_id_type=MESH,
        )

    run = rotate(
        slots, my_mod, query_ref, map_ref, out_basis_ref, in_basis_ref, eigen_ref,
        spread, right_ref, precond_ref, back_ref, damped, full, functools.partial(place, me),
    )
    sent = []
    for half in range(HALVES):
        run(half)
        if half == 0:
            pl.semaphore_wait(barrier, 1 + len(fars) + len(others))
        for slot in range(slots):
            for hop, far in enumerate(fars):
                copy = gather_copy(half, slot, me, far, far_send.at[half, slot, hop])
                copy.start()
                sent.append(copy)
            copy = gather_copy(half, slot, me, mate, mate_send.at[half, slot, 0])
            copy.start()
            sent.append(copy)

    size = 8 * per_row
    target = lax.broadcasted_iota(jnp.int32, (size, size), 0)
    source = lax.broadcasted_iota(jnp.int32, (size, size), 1)
    bits = columns.bit_length() - 1
    wanted = (target & 7) * per_row + ((target >> 3) & (columns - 1)) * slots + (target >> (3 + bits))
    sorter = (wanted == source).astype(jnp.float32).astype(jnp.bfloat16)

    def sort_segment(part):
        loads[part].wait()

        def step(i, carry):
            base = pl.multiple_of(i * 2 * size, 2 * size)
            pair = jnp.concatenate([staged[pl.ds(base, size), :], staged[pl.ds(base + size, size), :]], axis=1)
            done = jnp.dot(sorter, pair, preferred_element_type=jnp.float32)
            where = pl.ds(pl.multiple_of(i * 16, 16), 16)
            for slot in range(slots):
                for column in range(columns):
                    at = (slot * columns + column) * 8
                    both = jnp.concatenate([done[at:at + 8, :LANES], done[at:at + 8, LANES:]], axis=0)
                    train[slot, where, column * LANES:(column + 1) * LANES] = both.astype(jnp.bfloat16)
            return carry

        steps = segment // 16
        lax.fori_loop(0, steps // 4, lambda i, carry: [step(part * steps + i * 4 + k, carry) for k in range(4)][-1], 0)

    def forward(half, slot):
        for hop, far in enumerate(fars):
            gather_copy(half, slot, far, far, far_send.at[half, slot, hop]).wait_recv()
            copy = gather_copy(half, slot, far, mate, mate_send.at[half, slot, 1 + hop])
            copy.start()
            sent.append(copy)

    ids = lax.broadcasted_iota(jnp.int32, (total_q, total_q), 0)
    hot = (ids == owner_ref[...]).astype(jnp.float32).astype(jnp.bfloat16)
    own_ids = lax.broadcasted_iota(jnp.int32, (block, total_q), 0) + my_mod * block
    own_hot = (own_ids == owner_ref[...]).astype(jnp.float32).astype(jnp.bfloat16)

    def against(left, right):
        return lax.dot_general(left, right, (((1,), (1,)), ((), ())), preferred_element_type=jnp.float32)

    def accumulate(slot):
        for half in range(HALVES):
            for owner in [mate] + [far + 1 - 2 * core for far in fars]:
                gather_copy(half, slot, owner, mate, mate_send.at[half, slot, 0]).wait_recv()
        for part in range(raw.shape[0]):
            some = against(train[slot], full[slot, part * TILE:(part + 1) * TILE, :])
            raw[part] = some if slot == 0 else raw[part] + some

    def chunk(mod):
        return pl.ds(pl.multiple_of(mod * block, block), block)

    def sum_copy(tile, hop, to, landing):
        return pltpu.make_async_remote_copy(
            src_ref=outgoing.at[tile, chunk(to)],
            dst_ref=incoming.at[tile, landing],
            send_sem=sum_send.at[tile, hop],
            recv_sem=sum_recv.at[tile, landing],
            device_id={"mods": to},
            device_id_type=MESH,
        )

    for part in range(slots):
        sort_segment(part)
        forward(0, part)
    for slot in range(slots):
        forward(1, slot)
        if slot > 0:
            accumulate(slot - 1)
    accumulate(slots - 1)

    for tile in range(tiles):
        where = slice(tile * TILE, (tile + 1) * TILE)
        ordered = own = 0.0
        for part in range(raw.shape[0]):
            columns_of = slice(part * TILE, (part + 1) * TILE)
            high, low = split(raw[part, where, :])
            ordered = ordered + against(hot[:, columns_of], high)
            own = own + (against(own_hot[:, columns_of], high) + against(own_hot[:, columns_of], low))
        outgoing[tile] = ordered.astype(jnp.bfloat16)
        out_ref[:, where] = own
        for hop, mod in enumerate(others):
            copy = sum_copy(tile, hop, mod, mods - 2 - hop)
            copy.start()
            sent.append(copy)
    for tile in range(tiles):
        where = slice(tile * TILE, (tile + 1) * TILE)
        value = out_ref[:, where]
        for hop, mod in enumerate(others):
            sum_copy(tile, hop, mod, hop).wait_recv()
            value = value + incoming[tile, hop].astype(jnp.float32)
        out_ref[:, where] = value / counts_ref[:, where].astype(jnp.float32)
    for copy in sent:
        copy.wait_send()


def local(rows, mods, query_grads, train_grads, token_counts, query_owner, module_map, out_basis, in_basis, eigen_values):
    mine_q = query_grads.shape[0]
    train_rows, slots, feat = train_grads.shape
    columns = feat // LANES
    total_q = rows * mine_q
    tiles = train_rows // TILE
    block = total_q // mods
    staged = train_grads.reshape(train_rows, slots, columns, LANES).transpose(0, 2, 1, 3).reshape(-1, LANES)
    queries = query_grads.reshape(mine_q, slots, columns, LANES).transpose(0, 2, 1, 3).reshape(-1, LANES)
    owner = query_owner[None, :]
    counts = token_counts[None, :]
    vmem = pl.BlockSpec(memory_space=pltpu.VMEM)
    chips = rows // 2
    return pl.pallas_call(
        functools.partial(kernel, rows, mods),
        out_shape=jax.ShapeDtypeStruct((block, train_rows), jnp.float32),
        in_specs=[vmem, pl.BlockSpec(memory_space=pl.ANY), vmem, vmem, pl.BlockSpec(memory_space=pltpu.SMEM), vmem, vmem, vmem],
        out_specs=vmem,
        scratch_shapes=[
            pltpu.VMEM((FACTOR, FACTOR, LANES), jnp.float32),
            pltpu.VMEM((FACTOR, mine_q // HALVES, LANES), jnp.float32),
            pltpu.VMEM((FACTOR, mine_q // HALVES, LANES), jnp.float32),
            pltpu.VMEM((FACTOR, mine_q // HALVES, LANES), jnp.float32),
            pltpu.VMEM((FACTOR, LANES), jnp.float32),
            pltpu.VMEM(staged.shape, jnp.bfloat16),
            pltpu.VMEM((slots, train_rows, feat), jnp.bfloat16),
            pltpu.VMEM((slots, total_q, feat), jnp.bfloat16),
            pltpu.VMEM((total_q // TILE, train_rows, TILE), jnp.float32),
            pltpu.VMEM((tiles, total_q, TILE), jnp.bfloat16),
            pltpu.VMEM((tiles, mods - 1, block, TILE), jnp.bfloat16),
            pltpu.SemaphoreType.DMA((slots,)),
            pltpu.SemaphoreType.DMA((HALVES, slots, max(chips - 1, 1))),
            pltpu.SemaphoreType.DMA((HALVES, slots, chips)),
            pltpu.SemaphoreType.DMA((HALVES, slots, rows)),
            pltpu.SemaphoreType.DMA((tiles, mods - 1)),
            pltpu.SemaphoreType.DMA((tiles, mods - 1)),
        ],
        compiler_params=pltpu.CompilerParams(
            collective_id=0, has_side_effects=True, vmem_limit_bytes=56 * 1024 * 1024
        ),
        name="score",
    )(queries, staged, owner, counts, module_map, out_basis, in_basis, eigen_values)


def solution(mesh):
    in_specs = (
        P(("groups", "rows"), "mods", None),
        P(("groups", "rows"), "mods", None),
        P(("groups", "rows")),
        P("groups"),
        P(),
        P(),
        P(),
        P(),
    )
    out_specs = P(("groups", "mods"), "rows")
    body = functools.partial(local, mesh.shape["rows"], mesh.shape["mods"])
    return jax.shard_map(body, mesh=mesh, in_specs=in_specs, out_specs=out_specs, check_vma=False)
```

time: 51.6 us -> 48.5 us (0.940)
  Pallas kernels: 49.8 us -> 46.7 us
    pallas_call x1, Pallas kernels: 49.8 us -> 46.7 us  [local(): pl.pallas_call(functools.partial(kernel, rows, mods), out_shape=jax.Shape...]
where the time goes in v3:
time: 48.5 us; the launch traced here: 48.3 us
  Pallas kernels  46.7 us (96%)
  local copies, waits for them, and re-layouts  1.67 us (3%)
    pallas_call x1, Pallas kernels, local(): pl.pallas_call(functools.partial(kernel, rows, mods), out_shape=jax.Shape...  46.7 us
    unnamed x1, local copies, waits for them, and re-layouts  1.67 us

profile of v3, /device:TPU:0, one launch (start us, length us, event | category | flops | bytes accessed | tf_op | source)
XLA Modules:
  0.0 48.3 jit_solution(7910324541910050278)
XLA Ops:
  0.0 46.7 %score.1 = f32[64,1024]{1,0:T(8,128)} custom-call(f32[2048,128]{1,0:T(8,128)} %bitcast.13, bf16[32768,128]{1,0:T(8,128)(2,1)} %bitcast.12, s32[1,256]{1,0:T(1,128)} %bitcast.15, s32[1,1024]{1,0:T(1,128)} %bitcast.14, s32[16]{0:T(128)} %map_ref.1, f32[16,32,32]{2,1,0:T(8,128)} %out_basis_ref.1, f32[16,32,32]{2,1,0:T(8,128)} %in_basis_ref.1, f32[16,1024]{1,0:T(8,128)} %eigen_ref.1), custom_call_target="tpu_custom_call" | custom-call | tf_op jit(solution)/shard_map/score/pallas_call | solution.py:314
  46.7 1.7 %copy.12 = f32[64,1024]{1,0:T(8,128)} copy(f32[64,1024]{1,0:T(8,128)} %score.1) | data formatting | bytes 524288

commit v4 on v3

--- a/solution.py
+++ b/solution.py
@@ -85,18 +85,26 @@
 
     def run(half):
         start = half * count
+        grads = jnp.concatenate(
+            [
+                jnp.concatenate(
+                    [
+                        query_ref[pl.ds((start * columns + column) * slots + slot, count, stride=columns * slots), :]
+                        for slot in range(slots)
+                    ],
+                    axis=1,
+                )
+                for column in range(columns)
+            ],
+            axis=0,
+        )
+        high, low = split(grads)
+        size = columns * count
+        both = dot(jnp.concatenate([high, low], axis=0), block_high)
+        right = both[:size] + (both[size:] + dot(high, block_low))
         for column in range(columns):
-            grads = jnp.concatenate(
-                [
-                    query_ref[pl.ds((start * columns + column) * slots + slot, count, stride=columns * slots), :]
-                    for slot in range(slots)
-                ],
-                axis=1,
-            )
-            high, low = split(grads)
-            right = dot(high, block_high) + (dot(low, block_high) + dot(high, block_low))
             for o in range(group):
-                right_ref[column * group + o] = right[:, o * LANES:(o + 1) * LANES]
+                right_ref[column * group + o] = right[column * count:(column + 1) * count, o * LANES:(o + 1) * LANES]
 
         def forth(step, carry):
             p = step * together
@@ -125,12 +133,20 @@
 
         lax.fori_loop(0, FACTOR // together, back, 0)
 
+        value = jnp.concatenate(
+            [
+                jnp.concatenate([back_ref[column * group + o] for o in range(group)], axis=1)
+                for column in range(columns)
+            ],
+            axis=0,
+        )
+        both = turn(jnp.concatenate(split(value), axis=0))
+        result = (both[:size] + both[size:]).astype(jnp.bfloat16)
         for column in range(columns):
-            value = jnp.concatenate([back_ref[column * group + o] for o in range(group)], axis=1)
-            high, low = split(value)
-            result = (turn(high) + turn(low)).astype(jnp.bfloat16)
             for slot in range(slots):
-                full[slot, place(half), column * LANES:(column + 1) * LANES] = result[:, slot * LANES:(slot + 1) * LANES]
+                full[slot, place(half), column * LANES:(column + 1) * LANES] = result[
+                    column * count:(column + 1) * count, slot * LANES:(slot + 1) * LANES
+                ]
 
     return run
 

time: 48.5 us -> 42.6 us (0.88)
  Pallas kernels: 46.7 us -> 40.7 us
    pallas_call x1, Pallas kernels: 46.7 us -> 40.7 us  [local(): pl.pallas_call(functools.partial(kernel, rows, mods), out_shape=jax.Shape...]
where the time goes in v4:
time: 42.6 us; the launch traced here: 42.4 us
  Pallas kernels  40.7 us (96%)
  local copies, waits for them, and re-layouts  1.67 us (4%)
    pallas_call x1, Pallas kernels, local(): pl.pallas_call(functools.partial(kernel, rows, mods), out_shape=jax.Shape...  40.7 us
    unnamed x1, local copies, waits for them, and re-layouts  1.67 us

profile of v4, /device:TPU:0, one launch (start us, length us, event | category | flops | bytes accessed | tf_op | source)
XLA Modules:
  0.0 42.4 jit_solution(13749123555582244316)
XLA Ops:
  0.0 40.7 %score.1 = f32[64,1024]{1,0:T(8,128)} custom-call(f32[2048,128]{1,0:T(8,128)} %bitcast.13, bf16[32768,128]{1,0:T(8,128)(2,1)} %bitcast.12, s32[1,256]{1,0:T(1,128)} %bitcast.15, s32[1,1024]{1,0:T(1,128)} %bitcast.14, s32[16]{0:T(128)} %map_ref.1, f32[16,32,32]{2,1,0:T(8,128)} %out_basis_ref.1, f32[16,32,32]{2,1,0:T(8,128)} %in_basis_ref.1, f32[16,1024]{1,0:T(8,128)} %eigen_ref.1), custom_call_target="tpu_custom_call" | custom-call | tf_op jit(solution)/shard_map/score/pallas_call | solution.py:330
  40.8 1.7 %copy.12 = f32[64,1024]{1,0:T(8,128)} copy(f32[64,1024]{1,0:T(8,128)} %score.1) | data formatting | bytes 524288
